TPU v7x, 32 devices: a whole 2x2x4 slice. The times are simulated.
32 devices in a mesh: dp: 4 (over z), expert: 8 (over y, x, core).
Axes of the slice: x: 2, y: 2, z: 4, core: 2. Of those that a mesh axis runs over, the one named last changes fastest.
Arguments:
- tokens: bfloat16 [128, 7168], P(('dp', 'expert')), may hold values from -6 to 6
- routes: int32 [128, 2], P(('dp', 'expert')), may hold values from 0 to 7, all different within a row; in each aligned block of 4 rows (0 to 3, 4 to 7, ...) at most 2 rows name the same one
- gate_scores: float32 [128, 2], P(('dp', 'expert')), may hold values from 0.1 to 1
- w_gate: bfloat16 [8, 7168, 2048], P('expert', None, 'dp'), may hold values from -0.0625 to 0.0625
- w_up: bfloat16 [8, 7168, 2048], P('expert', None, 'dp'), may hold values from -0.0625 to 0.0625
- w_down: bfloat16 [8, 2048, 7168], P('expert', 'dp'), may hold values from -0.125 to 0.125
Outputs:
- mixed_out: bfloat16 [128, 7168], P(('dp', 'expert'))
Inputs may be any that keep to these rules, and one draw needn't show every extreme that they name: `routes`: each row names 2 different experts. In the rows of one device (aligned blocks of 4 rows) no expert is named by more than 2 rows, a bound that some block reaches.
All inputs are finite; a program needn't handle non-finite values.
Results may differ from a plain program's by a relative error of at most 0.0098.
Values may be sent and summed in bfloat16 or wider, within the bound.
A program may use at most 128 MiB of HBM per device.

v0:
```python
import jax
import jax.numpy as jnp
from jax import lax
from jax.sharding import PartitionSpec as P


def slots_of(route_ids, owners):
    matched = (route_ids[:, None] == jnp.arange(owners, dtype=jnp.int32)[None, :]).astype(jnp.int32)
    before = jnp.cumsum(matched, axis=0) - matched
    return jnp.sum(before * matched, axis=1)


def expert_rows(picked_rows, gate_mat, up_mat, down_mat):
    gate_act = jnp.dot(picked_rows, gate_mat, preferred_element_type=jnp.float32)
    up_act = jnp.dot(picked_rows, up_mat, preferred_element_type=jnp.float32)
    hidden = (jax.nn.silu(gate_act) * up_act).astype(jnp.bfloat16)
    return jnp.dot(hidden, down_mat, preferred_element_type=jnp.float32)


def shards(tokens, routes, gate_scores, w_gate, w_up, w_down):
    tok_rows, model_width = tokens.shape
    route_count = routes.shape[1]
    owners = lax.axis_size("expert")
    groups = lax.axis_size("dp")
    capacity = tok_rows // 4 + 1
    gate_mat, up_mat, down_mat = (w_gate[0], w_up[0], w_down[0])
    source = jnp.repeat(jnp.arange(tok_rows, dtype=jnp.int32), route_count)
    flat_ids = routes.reshape(-1)
    own_slots = slots_of(flat_ids, owners)
    target_row = flat_ids * capacity + own_slots
    outgoing = (
        jnp.zeros((owners * capacity, model_width), jnp.bfloat16).at[target_row].set(tokens[source])
    )
    arrived = lax.all_to_all(
        outgoing.reshape(owners, capacity, model_width),
        "expert",
        split_axis=0,
        concat_axis=0,
        tiled=True,
    )
    blocks = lax.all_gather(arrived[None], "dp", axis=0, tiled=True)
    block_shape = blocks.shape[:-1] + (model_width,)
    flat_out = expert_rows(blocks.reshape(-1, model_width), gate_mat, up_mat, down_mat)
    partial_value = flat_out.reshape(block_shape)
    returned = lax.all_to_all(partial_value, "expert", split_axis=1, concat_axis=1, tiled=True)
    all_routes, all_scores = (
        lax.all_gather(routes, "dp", axis=0, tiled=True),
        lax.all_gather(gate_scores, "dp", axis=0, tiled=True),
    )
    group_ids = all_routes.reshape(groups, tok_rows * route_count)
    group_slots = jax.vmap(lambda group_row: slots_of(group_row, owners))(group_ids)
    lookup = group_ids * capacity + group_slots
    picked = jnp.take_along_axis(
        returned.reshape(groups, owners * capacity, model_width), lookup[:, :, None], axis=1
    )
    weights = all_scores.reshape(groups, tok_rows, route_count)
    weighted = jnp.sum(
        picked.reshape(groups, tok_rows, route_count, model_width) * weights[..., None], axis=2
    )
    mixed_out = lax.psum_scatter(weighted, "dp", scatter_dimension=0, tiled=True)[0]
    return mixed_out.astype(jnp.bfloat16)


def solution(mesh):
    return jax.shard_map(
        shards,
        mesh=mesh,
        in_specs=(
            P(("dp", "expert"), None),
            P(("dp", "expert"), None),
            P(("dp", "expert"), None),
            P("expert", None, "dp"),
            P("expert", None, "dp"),
            P("expert", "dp", None),
        ),
        out_specs=P(("dp", "expert"), None),
        check_vma=False,
    )
```

profile of v0, /device:TPU:0, one launch (start us, length us, event | category | flops | bytes accessed | tf_op | source)
XLA Modules:
  0.0 111.4 jit_solution(11758337984328518183)
XLA Ops:
  0.0 0.7 broadcast_multiply_fusion.1
  0.7 0.8 copy.53
  1.8 0.2 select_reduce_fusion.1
  2.1 1.2 %scatter_custom_fusion = bf16[16,7168]{1,0:T(8,128)(2,1)S(1)} fusion(s32[8]{0:T(128)S(1)} %fusion.22, bf16[4,7168]{1,0:T(4,128)(2,1)S(1)} %copy-done, s32[1024]{0:T(1024)S(1)} %pad_clamp_fusion, bf16[]{:T(256)} %constant.32.clone.1), kind=kCustom, calls=%fused_computation.13 | custom fusion | bytes 229378 | tf_op jit(solution)/shard_map/scatter | solution.py:32
  3.4 11.6 %all_to_all.10 = bf16[8,2,7168]{2,1,0:T(2,128)(2,1)S(1)} all-to-all(bf16[8,2,7168]{2,1,0:T(2,128)(2,1)S(1)} %reshape.125), channel_id=1, replica_groups=mesh['dp'=4,'expert'=8] {'expert'}, dimensions={0} | all-to-all | bytes 458752 | tf_op jit(solution)/shard_map/all_to_all | solution.py:34
  15.0 21.8 %all-gather = bf16[32,2,7168]{2,1,0:T(2,128)(2,1)} all-gather(bf16[8,2,7168]{2,1,0:T(2,128)(2,1)S(1)} %all_to_all.10), channel_id=2, replica_groups=mesh['dp'=4,'expert'=8] {'dp'}, dimensions={0}, use_global_device_ids=true | all-gather | bytes 1146880 | tf_op jit(solution)/shard_map/all_gather | solution.py:41
  36.7 3.4 %reshape.126 = bf16[64,7168]{1,0:T(8,128)(2,1)} reshape(bf16[32,2,7168]{2,1,0:T(2,128)(2,1)} %all-gather) | data formatting | bytes 1835008 | tf_op jit(solution)/shard_map/reshape | solution.py:43
  40.1 4.9 %fusion.4 = f32[64,512]{1,0:T(8,128)S(1)} fusion(bf16[64,7168]{1,0:T(8,128)(2,1)} %reshape.126, bf16[1,7168,512]{2,1,0:T(8,128)(2,1)} %param.9), kind=kOutput, calls=%fused_computation.7 | convolution fusion | flops 469762048 | bytes 8388608 | tf_op jit(solution)/shard_map/dot_general | solution.py:14
  45.0 1.4 %fusion.9 = bf16[64,512]{1,0:T(8,128)(2,1)S(1)} fusion(bf16[64,7168]{1,0:T(8,128)(2,1)S(1)} %copy-done.1, bf16[1,7168,512]{2,1,0:T(8,128)(2,1)S(1)} %bitcast.40, f32[64,512]{1,0:T(8,128)S(1)} %fusion.4), kind=kOutput, calls=%fused_computation.10 | convolution fusion | flops 469958656 | bytes 8454144 | tf_op jit(solution)/shard_map/dot_general | solution.py:15
  46.5 4.5 %fusion = f32[4,8,2,7168]{3,1,2,0:T(8,128)S(1)} fusion(bf16[1,512,7168]{2,1,0:T(8,128)(2,1)} %param.11, bf16[4,8,2,512]{3,2,1,0:T(2,128)(2,1)S(1)} %dot_general.13), kind=kOutput, calls=%fused_computation.3 | convolution fusion | flops 469762048 | bytes 9240576 | tf_op jit(solution)/shard_map/dot_general | solution.py:17
  51.0 2.7 %copy.55 = f32[4,8,2,7168]{3,2,0,1:T(2,128)} copy(f32[4,8,2,7168]{3,1,2,0:T(8,128)S(1)} %fusion) | data formatting | bytes 3670016 | tf_op jit(solution)/shard_map/dot_general | solution.py:17
  53.6 3.6 %all-to-all-start.1 = ((f32[4,8,2,7168]{3,2,0,1:T(2,128)}), f32[4,8,2,7168]{3,2,0,1:T(2,128)S(1)}, u32[]{:S(2)}, u32[]{:S(2)}) async-start(f32[4,8,2,7168]{3,2,0,1:T(2,128)} %copy.55), calls=%async_computation.1 | async-start | bytes 3670016 | tf_op jit(solution)/shard_map/all_to_all | solution.py:45
  57.3 9.0 %all-gather.1 = s32[4,4,2]{1,2,0:T(2,128)S(1)} all-gather(s32[1,4,2]{1,2,0:T(2,128)S(1)} %bitcast.46), channel_id=1, replica_groups=mesh['dp'=4,'expert'=8] {'dp'}, dimensions={0}, use_global_device_ids=true | all-gather | bytes 160 | tf_op jit(solution)/shard_map/all_gather | solution.py:47
  66.3 8.3 %all-gather.2 = f32[4,4,2]{1,2,0:T(2,128)S(1)} all-gather(f32[1,4,2]{1,2,0:T(2,128)S(1)} %bitcast.47), channel_id=1, replica_groups=mesh['dp'=4,'expert'=8] {'dp'}, dimensions={0}, use_global_device_ids=true | all-gather | bytes 160 | tf_op jit(solution)/shard_map/all_gather | solution.py:48
  74.9 0.2 select_reduce_fusion
  75.7 0.6 dynamic-slice
  76.3 4.7 %all-to-all-done.1 = f32[4,8,2,7168]{3,2,0,1:T(2,128)S(1)} async-done(((f32[4,8,2,7168]{3,2,0,1:T(2,128)}), f32[4,8,2,7168]{3,2,0,1:T(2,128)S(1)}, u32[]{:S(2)}, u32[]{:S(2)}) %all-to-all-start.1) | async-done | bytes 1835040 | tf_op jit(solution)/shard_map/all_to_all | solution.py:45
  81.0 0.7 copy.56
  81.7 1.1 copy.59
  82.8 1.4 %gather_fusion = f32[32,7168]{1,0:T(8,128)S(1)} fusion(f32[4,16,7168]{2,1,0:T(8,128)S(1)} %copy.59, s32[32]{0:T(128)S(1)} %reshape.136), kind=kCustom, calls=%fused_computation.1 | custom fusion | bytes 1835264 | tf_op jit(solution)/shard_map/jit(take_along_axis)/gather | solution.py:53
  84.2 0.5 gather.11
  84.7 1.4 %multiply_reduce_fusion = f32[4,4,7168]{2,1,0:T(4,128)S(1)} fusion(f32[4,4,2,7168]{3,2,1,0:T(2,128)S(1)} %gather.11, pred[4,4,2]{2,1,0:T(4,128)(4,1)S(1)} %copy.51, f32[4,4,2]{2,1,0:T(4,128)S(1)} %copy.60), kind=kLoop, calls=%fused_computation.11 | loop fusion | flops 573440 | bytes 1376416 | tf_op jit(solution)/shard_map/reduce_sum | solution.py:57
  86.1 24.1 %all-reduce.2 = bf16[4,4,7168]{2,1,0:T(4,128)(2,1)S(1)} all-reduce(f32[4,4,7168]{2,1,0:T(4,128)S(1)} %multiply_reduce_fusion), channel_id=3, replica_groups=mesh['dp'=4,'expert'=8] {'dp'}, use_global_device_ids=true, to_apply=%region_6.7.clone | all-reduce | flops 114688 | bytes 688128
  110.2 1.2 %fusion.16 = bf16[4,7168]{1,0:T(4,128)(2,1)} fusion(bf16[4,4,7168]{2,1,0:T(4,128)(2,1)S(1)} %all-reduce.2, u32[]{:T(128)} %bitcast.18), kind=kLoop, calls=%fused_computation.17 | loop fusion | bytes 114692 | tf_op jit(solution)/shard_map/convert_element_type | solution.py:61
  (40 shorter events, 1.5 us)
Async XLA Ops:
  0.0 2.1 %copy-start = (bf16[4,7168]{1,0:T(4,128)(2,1)S(1)}, bf16[4,7168]{1,0:T(4,128)(2,1)}, u32[]{:S(2)}) copy-start(bf16[4,7168]{1,0:T(4,128)(2,1)} %param.6) | copy-start | bytes 172036
  36.7 8.3 %slice-start = ((s8[7340032]{0:T(1024)(128)(4,1)}), s8[3145728]{0:T(1024)(128)(4,1)S(1)}, s32[]{:S(2)}) async-start(s8[7340032]{0:T(1024)(128)(4,1)} %bitcast.39), calls=%async_computation.2 | async-start | bytes 6291456
  40.1 4.9 %slice-start.1 = ((s8[7340032]{0:T(1024)(128)(4,1)}), s8[4194304]{0:T(1024)(128)(4,1)S(1)}, s32[]{:S(2)}) async-start(s8[7340032]{0:T(1024)(128)(4,1)} %bitcast.39), calls=%async_computation.3 | async-start | bytes 8388608
  40.1 4.9 %copy-start.1 = (bf16[64,7168]{1,0:T(8,128)(2,1)S(1)}, bf16[64,7168]{1,0:T(8,128)(2,1)}, u32[]{:S(2)}) copy-start(bf16[64,7168]{1,0:T(8,128)(2,1)} %reshape.126) | copy-start | bytes 2752516
  46.5 10.8 %copy-start.2 = (s32[4,2]{0,1:T(2,128)S(1)}, s32[4,2]{0,1:T(2,128)}, u32[]{:S(2)}) copy-start(s32[4,2]{0,1:T(2,128)} %param.7) | copy-start | bytes 100
  46.5 19.8 %copy-start.3 = (f32[4,2]{0,1:T(2,128)S(1)}, f32[4,2]{0,1:T(2,128)}, u32[]{:S(2)}) copy-start(f32[4,2]{0,1:T(2,128)} %param.8) | copy-start | bytes 100
  46.5 29.3 %copy-start.4 = (u32[32]{0:T(128)S(1)}, u32[32]{0:T(128)}, u32[]{:S(2)}) copy-start(u32[32]{0:T(128)} %constant.58) | copy-start | bytes 388
  53.6 27.4 %all-to-all-start.1 = ((f32[4,8,2,7168]{3,2,0,1:T(2,128)}), f32[4,8,2,7168]{3,2,0,1:T(2,128)S(1)}, u32[]{:S(2)}, u32[]{:S(2)}) async-start(f32[4,8,2,7168]{3,2,0,1:T(2,128)} %copy.55), calls=%async_computation.1 | async-start | bytes 3670016 | tf_op jit(solution)/shard_map/all_to_all | solution.py:45
where the time goes:
time: 112 us; the launch traced here: 111 us
  blocking collectives  74.8 us (67%)
  local copies, waits for them, and re-layouts  14.7 us (13%)
  matrix products  10.7 us (10%)
  waiting for transfers between devices  4.69 us (4%)
  starting transfers between devices  3.59 us (3%)
  other arithmetic  2.76 us (2%)
    unnamed x1, blocking collectives  24.1 us
    all_gather x1, blocking collectives, shards(): blocks = lax.all_gather(arrived[None], 'dp', axis=0, tiled=True)  21.8 us
    all_to_all x1, blocking collectives, shards(): lax.all_to_all(outgoing.reshape(owners, capacity, model_width), 'expert',...  11.6 us
    all_gather x1, blocking collectives, shards(): lax.all_gather(routes, 'dp', axis=0, tiled=True)  9.03 us
    all_gather x1, blocking collectives, shards(): lax.all_gather(gate_scores, 'dp', axis=0, tiled=True)  8.32 us
    dot_general x1, matrix products, expert_rows(): jnp.dot(picked_rows, gate_mat, preferred_element_type=jnp.float32)  4.88 us
    all_to_all x1, waiting for transfers between devices, shards(): lax.all_to_all(partial_value, 'expert', split_axis=1, concat_axis=1, tile...  4.69 us
    dot_general x1, matrix products, expert_rows(): return jnp.dot(hidden, down_mat, preferred_element_type=jnp.float32)  4.48 us
  transfers between devices with their start and end apart: 1, of which 1 were waited for; matrix products, arithmetic and copies ran while one was open for 2% of the time, Pallas kernels for 0%

commit v1 on v0

v1 whole, which is shorter than its diff:
```python
import functools

import jax
import jax.numpy as jnp
from jax import lax
from jax.experimental import pallas as pl
from jax.experimental.pallas import tpu as pltpu
from jax.sharding import PartitionSpec as P

MESH = pl.DeviceIdType.MESH
F32, BF16 = jnp.float32, jnp.bfloat16


def divide(value, by):
    assert by & (by - 1) == 0
    return lax.shift_right_logical(value, jnp.int32(by.bit_length() - 1))


def modulo(value, by):
    assert by & (by - 1) == 0
    return lax.bitwise_and(value, jnp.int32(by - 1))


def kernel(
    sizes, tok, routes, scores, wg_hbm, wu_hbm, wd_hbm, out,
    wg, wu, wd, zbuf, mbuf, outg, arr, ret, back, sel_ref, comb_ref, gate, up, acc, zout, zin,
    wsem, zs, zr, ms, mr, ps, pr, rs, rr, os_, or_,
):
    groups, owners, rows, top, width, hidden, cap = sizes
    quarters = 16 // rows
    chunk = width // quarters
    per = groups * cap
    fold = max(1, 16 // per)
    tall = fold * per
    wide = width // fold
    parts = quarters // fold
    total, columns = owners * tall, groups * 16
    z, me = lax.axis_index("dp"), lax.axis_index("expert")

    def zpeer(i):
        return lax.rem(z + i, groups)

    def peer(i):
        return lax.rem(me + i, owners)

    barrier = pltpu.get_barrier_semaphore()

    @pl.loop(1, groups)
    def _(i):
        pl.semaphore_signal(barrier, inc=1, device_id=(zpeer(i), me), device_id_type=MESH)

    @pl.loop(1, owners)
    def _(i):
        pl.semaphore_signal(barrier, inc=1, device_id=(z, peer(i)), device_id_type=MESH)

    def weight_copies(p):
        for h in range(fold):
            span = pl.ds(h * wide + p * chunk, chunk)
            yield pltpu.make_async_copy(wg_hbm.at[0, span, :], wg.at[span, :], wsem.at[0, h, p])
            yield pltpu.make_async_copy(wu_hbm.at[0, span, :], wu.at[span, :], wsem.at[1, h, p])

    def down_copies(p):
        for h in range(fold):
            span = pl.ds(h * wide + p * chunk, chunk)
            yield pltpu.make_async_copy(wd_hbm.at[0, :, span], wd.at[:, span], wsem.at[2, h, p])

    for p in range(parts):
        for copy in weight_copies(p):
            copy.start()
    for p in range(parts):
        for copy in down_copies(p):
            copy.start()

    mine = tok[...].astype(F32)
    zbuf[z] = jnp.concatenate(
        [mine[:, q * chunk : (q + 1) * chunk] for q in range(quarters)], axis=0
    ).astype(BF16)
    pairs = rows * top
    for j in range(rows):
        for k in range(top):
            at = j * top + k
            mbuf[z, at : at + 1, :] = jnp.full((1, 128), routes[j, k], jnp.int32).astype(F32)
            mbuf[z, pairs + at : pairs + at + 1, :] = jnp.full((1, 128), scores[j, k], F32)

    pl.semaphore_wait(barrier, groups + owners - 2)

    def z_copy(block, to, of):
        return pltpu.make_async_remote_copy(
            zbuf.at[block], zbuf.at[block], zs.at[to], zr.at[of], (to, me), device_id_type=MESH)

    def m_copy(block, to, of):
        return pltpu.make_async_remote_copy(
            mbuf.at[block], mbuf.at[block], ms.at[to], mr.at[of], (to, me), device_id_type=MESH)

    @pl.loop(1, groups)
    def _(i):
        m_copy(z, zpeer(i), z).start()
        z_copy(z, zpeer(i), z).start()

    @pl.loop(1, groups)
    def _(i):
        m_copy(zpeer(i), zpeer(i), zpeer(i)).wait_recv()

    shape = (total, columns)
    r_at = lax.broadcasted_iota(jnp.int32, (total, 1), 0)
    c_at = lax.broadcasted_iota(jnp.int32, (1, columns), 1)
    e_r = divide(r_at, tall).astype(F32)
    h_r, z_r, s_r = divide(modulo(r_at, tall), per), divide(modulo(r_at, per), cap), modulo(r_at, cap)
    z_c, q_c, j_c = divide(c_at, 16), divide(modulo(c_at, 16), rows), modulo(c_at, rows)
    info = sum(
        jnp.where(z_c == g, mbuf[g][:, :columns], 0.0) for g in range(groups)
    )
    before = jnp.zeros(shape, F32)
    chosen = jnp.zeros(shape, F32)
    weight = jnp.zeros(shape, F32)
    for j in range(rows):
        match = jnp.zeros(shape, F32)
        score = jnp.zeros(shape, F32)
        for k in range(top):
            at = j * top + k
            same = info[at : at + 1, :] == e_r
            match = jnp.where(same, 1.0, match)
            score = jnp.where(same, info[pairs + at : pairs + at + 1, :], score)
        here = jnp.where((before == s_r.astype(F32)) & (j_c == j), match, 0.0)
        chosen = chosen + here
        weight = weight + here * score
        before = before + match
    for p in range(parts):
        fits = (z_r == z_c) & (q_c == h_r * parts + p)
        sel_ref[p] = jnp.where(fits, chosen, 0.0).astype(BF16)
        back_weight = jnp.transpose(jnp.where(fits, weight, 0.0))
        high = back_weight.astype(BF16)
        low = (back_weight - high.astype(F32)).astype(BF16)
        comb_ref[p] = jnp.concatenate([high, low], axis=0)

    @pl.loop(1, groups)
    def _(i):
        z_copy(zpeer(i), zpeer(i), zpeer(i)).wait_recv()

    def slots_copy(p, src, dst, to, of):
        span = pl.ds(p * chunk, chunk)
        return pltpu.make_async_remote_copy(
            outg.at[src, :, span], arr.at[dst, :, span], ps.at[p, to], pr.at[p, of],
            (z, to), device_id_type=MESH)

    tokens16 = zbuf[...].reshape(columns, chunk)
    for p in range(parts):
        span = pl.ds(p * chunk, chunk)
        picked = jnp.dot(sel_ref[p], tokens16, preferred_element_type=F32).astype(BF16)
        outg[:, :, span] = picked.reshape(owners, tall, chunk)

        @pl.loop(1, owners)
        def _(i, p=p):
            slots_copy(p, peer(i), me, peer(i), me).start()

        arr[me, :, span] = outg[me, :, span]

    some = min(owners, max(1, 128 // tall))
    blocks = owners // some
    for p in range(parts):
        span = pl.ds(p * chunk, chunk)
        for copy in weight_copies(p):
            copy.wait()

        @pl.loop(1, owners)
        def _(i, p=p):
            slots_copy(p, peer(i), peer(i), peer(i), peer(i)).wait_recv()

        @pl.loop(0, blocks)
        def _(b, p=p, span=span):
            first = b * some
            lhs = arr[pl.ds(first, some), :, span].reshape(some * tall, chunk)
            at = pl.ds(pl.multiple_of(first * per, some * per), some * per)
            for mat, into in ((wg, gate), (wu, up)):
                step = min(256, hidden)
                for n in range(0, hidden, step):
                    part = jnp.zeros((some, per, step), F32)
                    for h in range(fold):
                        res = jnp.dot(
                            lhs, mat[h * wide + p * chunk : h * wide + (p + 1) * chunk, n : n + step],
                            preferred_element_type=F32)
                        part = part + res.reshape(some, fold, per, step)[:, h]
                    part = part.reshape(some * per, step)
                    if p == 0:
                        into[at, n : n + step] = part
                    else:
                        into[at, n : n + step] += part

    def back_copy(p, src, dst, to, of):
        span = pl.ds(p * chunk, chunk)
        return pltpu.make_async_remote_copy(
            ret.at[src, :, span], back.at[dst, :, span], rs.at[p, to], rr.at[p, of],
            (z, to), device_id_type=MESH)

    for p in range(parts):
        span = pl.ds(p * chunk, chunk)
        for copy in down_copies(p):
            copy.wait()

        @pl.loop(0, blocks)
        def _(b, p=p):
            first = b * some
            at = pl.ds(pl.multiple_of(first * per, some * per), some * per)
            gate_act = gate[at, :]
            act = (gate_act / (1.0 + jnp.exp(-gate_act)) * up[at, :]).astype(BF16)
            step = 256
            for n in range(0, chunk, step):
                both = []
                for h in range(fold):
                    start = h * wide + p * chunk + n
                    res = jnp.dot(act, wd[:, start : start + step], preferred_element_type=F32)
                    both.append(res.reshape(some, per, step))
                ret[pl.ds(first, some), :, p * chunk + n : p * chunk + n + step] = jnp.concatenate(
                    both, axis=1).astype(BF16)

        @pl.loop(1, owners)
        def _(i, p=p):
            back_copy(p, peer(i), me, peer(i), me).start()

        back[me, :, span] = ret[me, :, span]

    for p in range(parts):
        @pl.loop(1, owners)
        def _(i, p=p):
            back_copy(p, peer(i), peer(i), peer(i), peer(i)).wait_recv()

        step = 256
        for n in range(0, chunk, step):
            rhs = back[:, :, p * chunk + n : p * chunk + n + step].reshape(total, step)
            res = jnp.dot(comb_ref[p], rhs, preferred_element_type=F32)
            res = res[:columns] + res[columns:]
            if p == 0:
                acc[:, n : n + step] = res
            else:
                acc[:, n : n + step] += res

    def sum_copy(src, dst, to, of):
        return pltpu.make_async_remote_copy(
            zout.at[src], zin.at[dst], os_.at[to], or_.at[of], (to, me), device_id_type=MESH)

    zout[...] = acc[...].astype(BF16).reshape(groups, 16, chunk)

    @pl.loop(1, groups)
    def _(i):
        sum_copy(zpeer(i), z, zpeer(i), z).start()

    own = acc[pl.ds(pl.multiple_of(z * 16, 16), 16), :]
    zin[z] = jnp.zeros((16, chunk), BF16)

    @pl.loop(1, groups)
    def _(i):
        sum_copy(zpeer(i), zpeer(i), zpeer(i), zpeer(i)).wait_recv()

    for g in range(groups):
        own = own + zin[g].astype(F32)
    for q in range(quarters):
        out[:, q * chunk : (q + 1) * chunk] = own[q * rows : (q + 1) * rows, :].astype(out.dtype)

    @pl.loop(1, groups)
    def _(i):
        m_copy(z, zpeer(i), z).wait_send()
        z_copy(z, zpeer(i), z).wait_send()
        sum_copy(zpeer(i), z, zpeer(i), z).wait_send()

    for p in range(parts):
        @pl.loop(1, owners)
        def _(i, p=p):
            slots_copy(p, peer(i), me, peer(i), me).wait_send()
            back_copy(p, peer(i), me, peer(i), me).wait_send()


def shards(tokens, routes, gate_scores, w_gate, w_up, w_down):
    rows, width = tokens.shape
    top = routes.shape[1]
    hidden = w_gate.shape[2]
    owners, groups = lax.axis_size("expert"), lax.axis_size("dp")
    cap = rows // 4 + 1
    quarters = 16 // rows
    chunk = width // quarters
    per = groups * cap
    fold = max(1, 16 // per)
    tall, wide, parts = fold * per, width // fold, quarters // fold
    total, columns = owners * tall, groups * 16
    sizes = (groups, owners, rows, top, width, hidden, cap)
    vmem = lambda shape, dtype=BF16: pltpu.VMEM(shape, dtype)
    dma = pltpu.SemaphoreType.DMA
    flops = 6 * owners * per * width * hidden
    return pl.pallas_call(
        functools.partial(kernel, sizes),
        out_shape=jax.ShapeDtypeStruct((rows, width), BF16),
        in_specs=[
            pl.BlockSpec(memory_space=pltpu.VMEM),
            pl.BlockSpec(memory_space=pltpu.SMEM),
            pl.BlockSpec(memory_space=pltpu.SMEM),
        ] + [pl.BlockSpec(memory_space=pl.ANY)] * 3,
        out_specs=pl.BlockSpec(memory_space=pltpu.VMEM),
        scratch_shapes=[
            vmem((width, hidden)), vmem((width, hidden)), vmem((hidden, width)),
            vmem((groups, 16, chunk)), vmem((groups, 2 * rows * top, 128), F32),
            vmem((owners, tall, wide)), vmem((owners, tall, wide)),
            vmem((owners, tall, wide)), vmem((owners, tall, wide)),
            vmem((parts, total, columns)), vmem((parts, 2 * columns, total)),
            vmem((owners * per, hidden), F32), vmem((owners * per, hidden), F32),
            vmem((columns, chunk), F32),
            vmem((groups, 16, chunk)), vmem((groups, 16, chunk)),
            dma((3, fold, parts)),
            dma((groups,)), dma((groups,)), dma((groups,)), dma((groups,)),
            dma((parts, owners)), dma((parts, owners)), dma((parts, owners)), dma((parts, owners)),
            dma((groups,)), dma((groups,)),
        ],
        compiler_params=pltpu.CompilerParams(
            collective_id=0, has_side_effects=True, vmem_limit_bytes=60 * 2**20),
        cost_estimate=pl.CostEstimate(
            flops=flops, bytes_accessed=6 * width * hidden, transcendentals=owners * per * hidden),
    )(tokens, routes, gate_scores, w_gate, w_up, w_down)


def solution(mesh):
    return jax.shard_map(
        shards,
        mesh=mesh,
        in_specs=(
            P(("dp", "expert"), None),
            P(("dp", "expert"), None),
            P(("dp", "expert"), None),
            P("expert", None, "dp"),
            P("expert", None, "dp"),
            P("expert", "dp", None),
        ),
        out_specs=P(("dp", "expert"), None),
        check_vma=False,
    )
```

time: 112 us -> 50 us (0.45)
  blocking collectives: 74.8 us -> 0 us
  Pallas kernels: 0 us -> 45.6 us
  matrix products: 10.7 us -> 0 us
  local copies, waits for them, and re-layouts: 14.7 us -> 4.12 us
  waiting for transfers between devices: 4.69 us -> 0 us
  starting transfers between devices: 3.59 us -> 0 us
  other arithmetic: 2.76 us -> 0 us
    pallas_call x0 -> x1, Pallas kernels: none -> 45.6 us  [shards(): pl.pallas_call(functools.partial(kernel, sizes), out_shape=jax.ShapeDtype...]
    all_gather x3 -> x0, blocking collectives: 39.1 us -> none  [the longest x1 21.8 us: shards(): blocks = lax.all_gather(arrived[None], 'dp', axis=0, tiled=True)]
    unnamed x1 -> x0, blocking collectives: 24.1 us -> none
    all_to_all x1 -> x0, blocking collectives: 11.6 us -> none  [shards(): lax.all_to_all(outgoing.reshape(owners, capacity, model_width), 'expert',...]
    dot_general x3 -> x0, matrix products: 10.7 us -> none  [the longest x1 4.88 us: expert_rows(): jnp.dot(picked_rows, gate_mat, preferred_element_type=jnp.float32)]
    all_to_all x1 -> x0, waiting for transfers between devices: 4.69 us -> none  [shards(): lax.all_to_all(partial_value, 'expert', split_axis=1, concat_axis=1, tile...]
    reshape x5 -> x0, local copies, waits for them, and re-layouts: 4.68 us -> none  [the longest x1 3.36 us: shards(): blocks.reshape(-1, model_width)]
    all_to_all x1 -> x0, starting transfers between devices: 3.59 us -> none  [shards(): lax.all_to_all(partial_value, 'expert', split_axis=1, concat_axis=1, tile...]
  transfers between devices with their start and end apart: 1 -> 0, of which waited for: 1 -> 0; matrix products, arithmetic and copies ran while one was open for 2% -> 0% of each run, Pallas kernels for 0% -> 0%
where the time goes in v1:
time: 50 us; the launch traced here: 49.7 us
  Pallas kernels  45.6 us (91%)
  local copies, waits for them, and re-layouts  4.12 us (8%)
    pallas_call x1, Pallas kernels, shards(): pl.pallas_call(functools.partial(kernel, sizes), out_shape=jax.ShapeDtype...  45.6 us
    unnamed x3, local copies, waits for them, and re-layouts  4.12 us

profile of v1, /device:TPU:0, one launch (start us, length us, event | category | flops | bytes accessed | tf_op | source)
XLA Modules:
  0.0 49.7 jit_solution(2752730372716535631)
XLA Ops:
  0.0 1.3 %copy.7.routes = s32[4,2]{1,0:T(4,128)} copy(s32[4,2]{0,1:T(2,128)} %param.7) | data formatting | bytes 64 | tf_op args[1]
  1.3 1.3 %copy.8.scores = f32[4,2]{1,0:T(4,128)} copy(f32[4,2]{0,1:T(2,128)} %param.8) | data formatting | bytes 64 | tf_op args[2]
  2.7 45.6 %shard_map.64 = bf16[4,7168]{1,0:T(4,128)(2,1)} custom-call(bf16[4,7168]{1,0:T(4,128)(2,1)} %tok.1, s32[4,2]{1,0:T(4,128)} %copy.7.routes, f32[4,2]{1,0:T(4,128)} %copy.8.scores, bf16[1,7168,512]{2,1,0:T(8,128)(2,1)} %wg_hbm.1, bf16[1,7168,512]{2,1,0:T(8,128)(2,1)} %wu_hbm.1, bf16[1,512,7168]{2,1,0:T(8,128)(2,1)} %wd_hbm.1), custom_call_target="tpu_custom_call" | custom-call | flops 1409286144 | bytes 22020096 | tf_op jit(solution)/shard_map/pallas_call | solution.py:288
  48.3 1.5 %copy.10 = bf16[4,7168]{1,0:T(4,128)(2,1)} copy(bf16[4,7168]{1,0:T(4,128)(2,1)} %shard_map.64) | data formatting | bytes 114688

commit v2 on v1

v2 whole, which is shorter than its diff:
```python
import functools

import jax
import jax.numpy as jnp
from jax import lax
from jax.experimental import pallas as pl
from jax.experimental.pallas import tpu as pltpu
from jax.sharding import PartitionSpec as P

MESH = pl.DeviceIdType.MESH
F32, BF16 = jnp.float32, jnp.bfloat16


def divide(value, by):
    assert by & (by - 1) == 0
    return lax.shift_right_logical(value, jnp.int32(by.bit_length() - 1))


def modulo(value, by):
    assert by & (by - 1) == 0
    return lax.bitwise_and(value, jnp.int32(by - 1))


def layout(sizes):
    groups, owners, rows, top, width, hidden, cap = sizes
    per = groups * cap
    fold = max(1, 16 // per)
    halves = 16 // (fold * rows)
    wide = width // fold
    small = 256 if wide % (halves * 256) == 0 else wide // halves
    chunk = halves * small
    return per, fold, fold * per, wide, halves, small, chunk, wide // chunk


def kernel(
    sizes, tok, routes, scores, wg_hbm, wu_hbm, wd_hbm, out,
    wg, wu, wd, zbuf, mbuf, outg, arr, ret, back, sel_ref, comb_ref, gate, up, act, acc, zout, zin,
    wsem, zs, zr, ms, mr, ps, pr, rs, rr, os_, or_,
):
    groups, owners, rows, top, width, hidden, cap = sizes
    per, fold, tall, wide, halves, small, chunk, parts = layout(sizes)
    total, columns = owners * tall, groups * 16
    z, me = lax.axis_index("dp"), lax.axis_index("expert")

    def zpeer(i):
        return lax.rem(z + i, groups)

    def peer(i):
        return lax.rem(me + i, owners)

    def span_of(p, base=0):
        return pl.ds(pl.multiple_of(base + p * chunk, chunk), chunk)

    barrier = pltpu.get_barrier_semaphore()

    @pl.loop(1, groups)
    def _(i):
        pl.semaphore_signal(barrier, inc=1, device_id=(zpeer(i), me), device_id_type=MESH)

    @pl.loop(1, owners)
    def _(i):
        pl.semaphore_signal(barrier, inc=1, device_id=(z, peer(i)), device_id_type=MESH)

    def weight_copies(p):
        for h in range(fold):
            span = span_of(p, h * wide)
            yield pltpu.make_async_copy(wg_hbm.at[0, span, :], wg.at[span, :], wsem.at[0, h, p])
            yield pltpu.make_async_copy(wu_hbm.at[0, span, :], wu.at[span, :], wsem.at[1, h, p])

    def down_copies(p):
        for h in range(fold):
            span = span_of(p, h * wide)
            yield pltpu.make_async_copy(wd_hbm.at[0, :, span], wd.at[:, span], wsem.at[2, h, p])

    mine = tok[...].astype(F32)
    for p in range(parts):
        pieces = []
        for h in range(fold):
            for u in range(halves):
                start = h * wide + p * chunk + u * small
                pieces.append(mine[:, start : start + small])
        zbuf[p, z] = jnp.concatenate(pieces, axis=0).astype(BF16)
    pairs = rows * top
    for j in range(rows):
        for k in range(top):
            at = j * top + k
            mbuf[z, at : at + 1, :] = jnp.full((1, 128), routes[k, j], jnp.int32).astype(F32)
            mbuf[z, pairs + at : pairs + at + 1, :] = jnp.full((1, 128), scores[k, j], F32)

    pl.semaphore_wait(barrier, groups + owners - 2)

    def z_copy(p, block, to, of):
        return pltpu.make_async_remote_copy(
            zbuf.at[p, block], zbuf.at[p, block], zs.at[p, to], zr.at[p, of],
            (to, me), device_id_type=MESH)

    def m_copy(block, to, of):
        return pltpu.make_async_remote_copy(
            mbuf.at[block], mbuf.at[block], ms.at[to], mr.at[of], (to, me), device_id_type=MESH)

    @pl.loop(1, groups)
    def _(i):
        m_copy(z, zpeer(i), z).start()

    @pl.loop(0, parts)
    def _(p):
        @pl.loop(1, groups)
        def _(i):
            z_copy(p, z, zpeer(i), z).start()

    @pl.loop(0, parts)
    def _(p):
        for copy in weight_copies(p):
            copy.start()

    @pl.loop(0, parts)
    def _(p):
        for copy in down_copies(p):
            copy.start()

    gate[...] = jnp.zeros_like(gate)
    up[...] = jnp.zeros_like(up)

    @pl.loop(1, groups)
    def _(i):
        m_copy(zpeer(i), zpeer(i), zpeer(i)).wait_recv()

    shape = (total, columns)
    r_at = lax.broadcasted_iota(jnp.int32, (total, 1), 0)
    c_at = lax.broadcasted_iota(jnp.int32, (1, columns), 1)
    e_r = divide(r_at, tall).astype(F32)
    h_r, z_r, s_r = divide(modulo(r_at, tall), per), divide(modulo(r_at, per), cap), modulo(r_at, cap)
    z_c, q_c, j_c = divide(c_at, 16), divide(modulo(c_at, 16), rows), modulo(c_at, rows)
    info = sum(
        jnp.where(z_c == g, mbuf[g][:, :columns], 0.0) for g in range(groups)
    )
    before = jnp.zeros(shape, F32)
    chosen = jnp.zeros(shape, F32)
    weight = jnp.zeros(shape, F32)
    for j in range(rows):
        match = jnp.zeros(shape, F32)
        score = jnp.zeros(shape, F32)
        for k in range(top):
            at = j * top + k
            same = info[at : at + 1, :] == e_r
            match = jnp.where(same, 1.0, match)
            score = jnp.where(same, info[pairs + at : pairs + at + 1, :], score)
        here = jnp.where((before == s_r.astype(F32)) & (j_c == j), match, 0.0)
        chosen = chosen + here
        weight = weight + here * score
        before = before + match
    for u in range(halves):
        fits = (z_r == z_c) & (q_c == h_r * halves + u)
        sel_ref[u] = jnp.where(fits, chosen, 0.0).astype(BF16)
        back_weight = jnp.transpose(jnp.where(fits, weight, 0.0))
        high = back_weight.astype(BF16)
        low = (back_weight - high.astype(F32)).astype(BF16)
        comb_ref[u] = jnp.concatenate([high, low], axis=0)

    def slots_copy(p, src, dst, to, of):
        span = span_of(p)
        return pltpu.make_async_remote_copy(
            outg.at[src, :, span], arr.at[dst, :, span], ps.at[p, to], pr.at[p, of],
            (z, to), device_id_type=MESH)

    @pl.loop(0, parts)
    def _(p):
        @pl.loop(1, groups)
        def _(i):
            z_copy(p, zpeer(i), zpeer(i), zpeer(i)).wait_recv()

        tokens16 = zbuf[p].reshape(columns, small)
        for u in range(halves):
            picked = jnp.dot(sel_ref[u], tokens16, preferred_element_type=F32).astype(BF16)
            outg[:, :, pl.ds(pl.multiple_of(p * chunk + u * small, small), small)] = picked.reshape(
                owners, tall, small)

        @pl.loop(1, owners)
        def _(i):
            slots_copy(p, peer(i), me, peer(i), me).start()

        arr[me, :, span_of(p)] = outg[me, :, span_of(p)]

    some = min(owners, max(1, 128 // tall))
    blocks = owners // some

    @pl.loop(0, parts)
    def _(p):
        for copy in weight_copies(p):
            copy.wait()

        @pl.loop(1, owners)
        def _(i):
            slots_copy(p, peer(i), peer(i), peer(i), peer(i)).wait_recv()

        @pl.loop(0, blocks)
        def _(b):
            first = b * some
            lhs = arr[pl.ds(first, some), :, span_of(p)].reshape(some * tall, chunk)
            at = pl.ds(pl.multiple_of(first * per, some * per), some * per)
            step = min(256, hidden)
            for mat, into in ((wg, gate), (wu, up)):
                for n in range(0, hidden, step):
                    part = into[at, n : n + step].reshape(some, per, step)
                    for h in range(fold):
                        res = jnp.dot(
                            lhs, mat[span_of(p, h * wide), n : n + step],
                            preferred_element_type=F32)
                        part = part + res.reshape(some, fold, per, step)[:, h]
                    into[at, n : n + step] = part.reshape(some * per, step)

    gate_act = gate[...]
    act[...] = (gate_act / (1.0 + jnp.exp(-gate_act)) * up[...]).astype(BF16)

    def back_copy(p, src, dst, to, of):
        span = span_of(p)
        return pltpu.make_async_remote_copy(
            ret.at[src, :, span], back.at[dst, :, span], rs.at[p, to], rr.at[p, of],
            (z, to), device_id_type=MESH)

    @pl.loop(0, parts)
    def _(p):
        for copy in down_copies(p):
            copy.wait()

        @pl.loop(0, blocks)
        def _(b):
            first = b * some
            at = pl.ds(pl.multiple_of(first * per, some * per), some * per)
            lhs = act[at, :]
            both = [
                jnp.dot(lhs, wd[:, span_of(p, h * wide)], preferred_element_type=F32).reshape(
                    some, per, chunk)
                for h in range(fold)
            ]
            ret[pl.ds(first, some), :, span_of(p)] = jnp.concatenate(both, axis=1).astype(BF16)

        @pl.loop(1, owners)
        def _(i):
            back_copy(p, peer(i), me, peer(i), me).start()

        back[me, :, span_of(p)] = ret[me, :, span_of(p)]

    def sum_copy(p, src, dst, to, of):
        return pltpu.make_async_remote_copy(
            zout.at[p, src], zin.at[p, dst], os_.at[p, to], or_.at[p, of],
            (to, me), device_id_type=MESH)

    @pl.loop(0, parts)
    def _(p):
        @pl.loop(1, owners)
        def _(i):
            back_copy(p, peer(i), peer(i), peer(i), peer(i)).wait_recv()

        mixed = jnp.zeros((columns, small), F32)
        for u in range(halves):
            rhs = back[:, :, pl.ds(pl.multiple_of(p * chunk + u * small, small), small)]
            res = jnp.dot(comb_ref[u], rhs.reshape(total, small), preferred_element_type=F32)
            mixed = mixed + res[:columns] + res[columns:]
        acc[p] = mixed
        zout[p] = mixed.astype(BF16).reshape(groups, 16, small)

        @pl.loop(1, groups)
        def _(i):
            sum_copy(p, zpeer(i), z, zpeer(i), z).start()

        zin[p, z] = jnp.zeros((16, small), BF16)

    for p in range(parts):
        @pl.loop(1, groups)
        def _(i, p=p):
            sum_copy(p, zpeer(i), zpeer(i), zpeer(i), zpeer(i)).wait_recv()

        own = acc[p, pl.ds(pl.multiple_of(z * 16, 16), 16), :]
        for g in range(groups):
            own = own + zin[p, g].astype(F32)
        for h in range(fold):
            for u in range(halves):
                start, row = h * wide + p * chunk + u * small, (h * halves + u) * rows
                out[:, start : start + small] = own[row : row + rows, :].astype(out.dtype)

    @pl.loop(1, groups)
    def _(i):
        m_copy(z, zpeer(i), z).wait_send()

    @pl.loop(0, parts)
    def _(p):
        @pl.loop(1, groups)
        def _(i):
            z_copy(p, z, zpeer(i), z).wait_send()
            sum_copy(p, zpeer(i), z, zpeer(i), z).wait_send()

        @pl.loop(1, owners)
        def _(i):
            slots_copy(p, peer(i), me, peer(i), me).wait_send()
            back_copy(p, peer(i), me, peer(i), me).wait_send()


def shards(tokens, routes, gate_scores, w_gate, w_up, w_down):
    rows, width = tokens.shape
    top = routes.shape[1]
    hidden = w_gate.shape[2]
    owners, groups = lax.axis_size("expert"), lax.axis_size("dp")
    cap = rows // 4 + 1
    sizes = (groups, owners, rows, top, width, hidden, cap)
    per, fold, tall, wide, halves, small, chunk, parts = layout(sizes)
    total, columns = owners * tall, groups * 16
    vmem = lambda shape, dtype=BF16: pltpu.VMEM(shape, dtype)
    dma = pltpu.SemaphoreType.DMA
    flops = 6 * owners * per * width * hidden
    return pl.pallas_call(
        functools.partial(kernel, sizes),
        out_shape=jax.ShapeDtypeStruct((rows, width), BF16),
        in_specs=[
            pl.BlockSpec(memory_space=pltpu.VMEM),
            pl.BlockSpec(memory_space=pltpu.SMEM),
            pl.BlockSpec(memory_space=pltpu.SMEM),
        ] + [pl.BlockSpec(memory_space=pl.ANY)] * 3,
        out_specs=pl.BlockSpec(memory_space=pltpu.VMEM),
        scratch_shapes=[
            vmem((width, hidden)), vmem((width, hidden)), vmem((hidden, width)),
            vmem((parts, groups, 16, small)), vmem((groups, 2 * rows * top, 128), F32),
            vmem((owners, tall, wide)), vmem((owners, tall, wide)),
            vmem((owners, tall, wide)), vmem((owners, tall, wide)),
            vmem((halves, total, columns)), vmem((halves, 2 * columns, total)),
            vmem((owners * per, hidden), F32), vmem((owners * per, hidden), F32),
            vmem((owners * per, hidden)), vmem((parts, columns, small), F32),
            vmem((parts, groups, 16, small)), vmem((parts, groups, 16, small)),
            dma((3, fold, parts)),
            dma((parts, groups)), dma((parts, groups)), dma((groups,)), dma((groups,)),
            dma((parts, owners)), dma((parts, owners)), dma((parts, owners)), dma((parts, owners)),
            dma((parts, groups)), dma((parts, groups)),
        ],
        compiler_params=pltpu.CompilerParams(
            collective_id=0, has_side_effects=True, vmem_limit_bytes=60 * 2**20),
        cost_estimate=pl.CostEstimate(
            flops=flops, bytes_accessed=6 * width * hidden, transcendentals=owners * per * hidden),
    )(tokens, routes.T, gate_scores.T, w_gate, w_up, w_down)


def solution(mesh):
    return jax.shard_map(
        shards,
        mesh=mesh,
        in_specs=(
            P(("dp", "expert"), None),
            P(("dp", "expert"), None),
            P(("dp", "expert"), None),
            P("expert", None, "dp"),
            P("expert", None, "dp"),
            P("expert", "dp", None),
        ),
        out_specs=P(("dp", "expert"), None),
        check_vma=False,
    )
```

time: 50 us -> 44 us (0.88)
  Pallas kernels: 45.6 us -> 42.4 us
  local copies, waits for them, and re-layouts: 4.12 us -> 1.46 us
    pallas_call x1, Pallas kernels: 45.6 us -> 42.4 us  [shards(): pl.pallas_call(functools.partial(kernel, sizes), out_shape=jax.ShapeDtype...]
    unnamed x3 -> x1, local copies, waits for them, and re-layouts: 4.12 us -> 1.46 us
where the time goes in v2:
time: 44 us; the launch traced here: 43.8 us
  Pallas kernels  42.4 us (96%)
  local copies, waits for them, and re-layouts  1.46 us (3%)
    pallas_call x1, Pallas kernels, shards(): pl.pallas_call(functools.partial(kernel, sizes), out_shape=jax.ShapeDtype...  42.4 us
    unnamed x1, local copies, waits for them, and re-layouts  1.46 us

profile of v2, /device:TPU:0, one launch (start us, length us, event | category | flops | bytes accessed | tf_op | source)
XLA Modules:
  0.0 43.8 jit_solution(12618201647275364934)
XLA Ops:
  0.0 42.4 %shard_map.64 = bf16[4,7168]{1,0:T(4,128)(2,1)} custom-call(bf16[4,7168]{1,0:T(4,128)(2,1)} %tok.1, s32[2,4]{1,0:T(2,128)} %bitcast.2, f32[2,4]{1,0:T(2,128)} %bitcast.3, bf16[1,7168,512]{2,1,0:T(8,128)(2,1)} %wg_hbm.1, bf16[1,7168,512]{2,1,0:T(8,128)(2,1)} %wu_hbm.1, bf16[1,512,7168]{2,1,0:T(8,128)(2,1)} %wd_hbm.1), custom_call_target="tpu_custom_call" | custom-call | flops 1409286144 | bytes 22020096 | tf_op jit(solution)/shard_map/pallas_call | solution.py:311
  42.4 1.5 %copy.8 = bf16[4,7168]{1,0:T(4,128)(2,1)} copy(bf16[4,7168]{1,0:T(4,128)(2,1)} %shard_map.64) | data formatting | bytes 114688

commit v3 on v2

--- a/solution.py
+++ b/solution.py
@@ -42,35 +42,21 @@
     total, columns = owners * tall, groups * 16
     z, me = lax.axis_index("dp"), lax.axis_index("expert")
 
-    def zpeer(i):
-        return lax.rem(z + i, groups)
-
-    def peer(i):
-        return lax.rem(me + i, owners)
+    zpeers = [modulo(z + i, groups) for i in range(1, groups)]
+    peers = [modulo(me + i, owners) for i in range(1, owners)]
 
     def span_of(p, base=0):
         return pl.ds(pl.multiple_of(base + p * chunk, chunk), chunk)
 
     barrier = pltpu.get_barrier_semaphore()
 
-    @pl.loop(1, groups)
-    def _(i):
-        pl.semaphore_signal(barrier, inc=1, device_id=(zpeer(i), me), device_id_type=MESH)
-
-    @pl.loop(1, owners)
-    def _(i):
-        pl.semaphore_signal(barrier, inc=1, device_id=(z, peer(i)), device_id_type=MESH)
-
-    def weight_copies(p):
-        for h in range(fold):
-            span = span_of(p, h * wide)
-            yield pltpu.make_async_copy(wg_hbm.at[0, span, :], wg.at[span, :], wsem.at[0, h, p])
-            yield pltpu.make_async_copy(wu_hbm.at[0, span, :], wu.at[span, :], wsem.at[1, h, p])
-
-    def down_copies(p):
-        for h in range(fold):
-            span = span_of(p, h * wide)
-            yield pltpu.make_async_copy(wd_hbm.at[0, :, span], wd.at[:, span], wsem.at[2, h, p])
+    for to in zpeers:
+        pl.semaphore_signal(barrier, inc=1, device_id=(to, me), device_id_type=MESH)
+    for to in peers:
+        pl.semaphore_signal(barrier, inc=1, device_id=(z, to), device_id_type=MESH)
+
+    def arrive(ref, sem):
+        pltpu.make_async_copy(ref, ref, sem).wait()
 
     mine = tok[...].astype(F32)
     for p in range(parts):
@@ -89,41 +75,23 @@
 
     pl.semaphore_wait(barrier, groups + owners - 2)
 
-    def z_copy(p, block, to, of):
-        return pltpu.make_async_remote_copy(
-            zbuf.at[p, block], zbuf.at[p, block], zs.at[p, to], zr.at[p, of],
-            (to, me), device_id_type=MESH)
-
-    def m_copy(block, to, of):
-        return pltpu.make_async_remote_copy(
-            mbuf.at[block], mbuf.at[block], ms.at[to], mr.at[of], (to, me), device_id_type=MESH)
-
-    @pl.loop(1, groups)
-    def _(i):
-        m_copy(z, zpeer(i), z).start()
-
-    @pl.loop(0, parts)
-    def _(p):
-        @pl.loop(1, groups)
-        def _(i):
-            z_copy(p, z, zpeer(i), z).start()
-
-    @pl.loop(0, parts)
-    def _(p):
-        for copy in weight_copies(p):
-            copy.start()
-
-    @pl.loop(0, parts)
-    def _(p):
-        for copy in down_copies(p):
-            copy.start()
+    for to in zpeers:
+        pltpu.make_async_remote_copy(
+            mbuf.at[z], mbuf.at[z], ms, mr, (to, me), device_id_type=MESH).start()
+    for p in range(parts):
+        for to in zpeers:
+            pltpu.make_async_remote_copy(
+                zbuf.at[p, z], zbuf.at[p, z], zs, zr.at[p], (to, me), device_id_type=MESH).start()
+    for at, (src, dst) in enumerate(((wg_hbm, wg), (wu_hbm, wu), (wd_hbm, wd))):
+        piece = dst.shape[0] // 4
+        for i in range(4):
+            span = pl.ds(i * piece, piece)
+            pltpu.make_async_copy(src.at[0, span, :], dst.at[span, :], wsem.at[at]).start()
 
     gate[...] = jnp.zeros_like(gate)
     up[...] = jnp.zeros_like(up)
 
-    @pl.loop(1, groups)
-    def _(i):
-        m_copy(zpeer(i), zpeer(i), zpeer(i)).wait_recv()
+    arrive(mbuf.at[pl.ds(0, groups - 1)], mr)
 
     shape = (total, columns)
     r_at = lax.broadcasted_iota(jnp.int32, (total, 1), 0)
@@ -157,41 +125,32 @@
         low = (back_weight - high.astype(F32)).astype(BF16)
         comb_ref[u] = jnp.concatenate([high, low], axis=0)
 
-    def slots_copy(p, src, dst, to, of):
-        span = span_of(p)
-        return pltpu.make_async_remote_copy(
-            outg.at[src, :, span], arr.at[dst, :, span], ps.at[p, to], pr.at[p, of],
-            (z, to), device_id_type=MESH)
-
-    @pl.loop(0, parts)
-    def _(p):
-        @pl.loop(1, groups)
-        def _(i):
-            z_copy(p, zpeer(i), zpeer(i), zpeer(i)).wait_recv()
-
+    @pl.loop(0, parts)
+    def _(p):
+        arrive(zbuf.at[p, pl.ds(0, groups - 1)], zr.at[p])
         tokens16 = zbuf[p].reshape(columns, small)
         for u in range(halves):
             picked = jnp.dot(sel_ref[u], tokens16, preferred_element_type=F32).astype(BF16)
             outg[:, :, pl.ds(pl.multiple_of(p * chunk + u * small, small), small)] = picked.reshape(
                 owners, tall, small)
 
-        @pl.loop(1, owners)
-        def _(i):
-            slots_copy(p, peer(i), me, peer(i), me).start()
+        span = span_of(p)
+        for to in peers:
+            pltpu.make_async_remote_copy(
+                outg.at[to, :, span], arr.at[me, :, span], ps, pr.at[p],
+                (z, to), device_id_type=MESH).start()
 
         arr[me, :, span_of(p)] = outg[me, :, span_of(p)]
 
     some = min(owners, max(1, 128 // tall))
     blocks = owners // some
 
-    @pl.loop(0, parts)
-    def _(p):
-        for copy in weight_copies(p):
-            copy.wait()
-
-        @pl.loop(1, owners)
-        def _(i):
-            slots_copy(p, peer(i), peer(i), peer(i), peer(i)).wait_recv()
+    arrive(wg, wsem.at[0])
+    arrive(wu, wsem.at[1])
+
+    @pl.loop(0, parts)
+    def _(p):
+        arrive(arr.at[pl.ds(0, owners - 1), :, span_of(p)], pr.at[p])
 
         @pl.loop(0, blocks)
         def _(b):
@@ -212,17 +171,10 @@
     gate_act = gate[...]
     act[...] = (gate_act / (1.0 + jnp.exp(-gate_act)) * up[...]).astype(BF16)
 
-    def back_copy(p, src, dst, to, of):
-        span = span_of(p)
-        return pltpu.make_async_remote_copy(
-            ret.at[src, :, span], back.at[dst, :, span], rs.at[p, to], rr.at[p, of],
-            (z, to), device_id_type=MESH)
-
-    @pl.loop(0, parts)
-    def _(p):
-        for copy in down_copies(p):
-            copy.wait()
-
+    arrive(wd, wsem.at[2])
+
+    @pl.loop(0, parts)
+    def _(p):
         @pl.loop(0, blocks)
         def _(b):
             first = b * some
@@ -235,23 +187,21 @@
             ]
             ret[pl.ds(first, some), :, span_of(p)] = jnp.concatenate(both, axis=1).astype(BF16)
 
-        @pl.loop(1, owners)
-        def _(i):
-            back_copy(p, peer(i), me, peer(i), me).start()
+        span = span_of(p)
+        for to in peers:
+            pltpu.make_async_remote_copy(
+                ret.at[to, :, span], back.at[me, :, span], rs, rr.at[p],
+                (z, to), device_id_type=MESH).start()
 
         back[me, :, span_of(p)] = ret[me, :, span_of(p)]
 
-    def sum_copy(p, src, dst, to, of):
-        return pltpu.make_async_remote_copy(
-            zout.at[p, src], zin.at[p, dst], os_.at[p, to], or_.at[p, of],
-            (to, me), device_id_type=MESH)
-
-    @pl.loop(0, parts)
-    def _(p):
-        @pl.loop(1, owners)
-        def _(i):
-            back_copy(p, peer(i), peer(i), peer(i), peer(i)).wait_recv()
-
+    arrive(mbuf.at[pl.ds(0, groups - 1)], ms)
+    arrive(zbuf.at[:, pl.ds(0, groups - 1)], zs)
+    arrive(outg.at[pl.ds(0, owners - 1)], ps)
+
+    @pl.loop(0, parts)
+    def _(p):
+        arrive(back.at[pl.ds(0, owners - 1), :, span_of(p)], rr.at[p])
         mixed = jnp.zeros((columns, small), F32)
         for u in range(halves):
             rhs = back[:, :, pl.ds(pl.multiple_of(p * chunk + u * small, small), small)]
@@ -260,17 +210,15 @@
         acc[p] = mixed
         zout[p] = mixed.astype(BF16).reshape(groups, 16, small)
 
-        @pl.loop(1, groups)
-        def _(i):
-            sum_copy(p, zpeer(i), z, zpeer(i), z).start()
+        for to in zpeers:
+            pltpu.make_async_remote_copy(
+                zout.at[p, to], zin.at[p, z], os_, or_.at[p], (to, me), device_id_type=MESH).start()
 
         zin[p, z] = jnp.zeros((16, small), BF16)
 
+    arrive(ret.at[pl.ds(0, owners - 1)], rs)
     for p in range(parts):
-        @pl.loop(1, groups)
-        def _(i, p=p):
-            sum_copy(p, zpeer(i), zpeer(i), zpeer(i), zpeer(i)).wait_recv()
-
+        arrive(zin.at[p, pl.ds(0, groups - 1)], or_.at[p])
         own = acc[p, pl.ds(pl.multiple_of(z * 16, 16), 16), :]
         for g in range(groups):
             own = own + zin[p, g].astype(F32)
@@ -279,21 +227,7 @@
                 start, row = h * wide + p * chunk + u * small, (h * halves + u) * rows
                 out[:, start : start + small] = own[row : row + rows, :].astype(out.dtype)
 
-    @pl.loop(1, groups)
-    def _(i):
-        m_copy(z, zpeer(i), z).wait_send()
-
-    @pl.loop(0, parts)
-    def _(p):
-        @pl.loop(1, groups)
-        def _(i):
-            z_copy(p, z, zpeer(i), z).wait_send()
-            sum_copy(p, zpeer(i), z, zpeer(i), z).wait_send()
-
-        @pl.loop(1, owners)
-        def _(i):
-            slots_copy(p, peer(i), me, peer(i), me).wait_send()
-            back_copy(p, peer(i), me, peer(i), me).wait_send()
+    arrive(zout.at[:, pl.ds(0, groups - 1)], os_)
 
 
 def shards(tokens, routes, gate_scores, w_gate, w_up, w_down):
@@ -326,10 +260,8 @@
             vmem((owners * per, hidden), F32), vmem((owners * per, hidden), F32),
             vmem((owners * per, hidden)), vmem((parts, columns, small), F32),
             vmem((parts, groups, 16, small)), vmem((parts, groups, 16, small)),
-            dma((3, fold, parts)),
-            dma((parts, groups)), dma((parts, groups)), dma((groups,)), dma((groups,)),
-            dma((parts, owners)), dma((parts, owners)), dma((parts, owners)), dma((parts, owners)),
-            dma((parts, groups)), dma((parts, groups)),
+            dma((3,)), dma, dma((parts,)), dma, dma,
+            dma, dma((parts,)), dma, dma((parts,)), dma, dma((parts,)),
         ],
         compiler_params=pltpu.CompilerParams(
             collective_id=0, has_side_effects=True, vmem_limit_bytes=60 * 2**20),

time: 44 us -> 40 us (0.909)
  Pallas kernels: 42.4 us -> 38.4 us
    pallas_call x1, Pallas kernels: 42.4 us -> 38.4 us  [shards(): pl.pallas_call(functools.partial(kernel, sizes), out_shape=jax.ShapeDtype...]
where the time goes in v3:
time: 40 us; the launch traced here: 39.8 us
  Pallas kernels  38.4 us (96%)
  local copies, waits for them, and re-layouts  1.46 us (4%)
    pallas_call x1, Pallas kernels, shards(): pl.pallas_call(functools.partial(kernel, sizes), out_shape=jax.ShapeDtype...  38.4 us
    unnamed x1, local copies, waits for them, and re-layouts  1.46 us

profile of v3, /device:TPU:0, one launch (start us, length us, event | category | flops | bytes accessed | tf_op | source)
XLA Modules:
  0.0 39.8 jit_solution(10131096709505399025)
XLA Ops:
  0.0 38.4 %shard_map.64 = bf16[4,7168]{1,0:T(4,128)(2,1)} custom-call(bf16[4,7168]{1,0:T(4,128)(2,1)} %tok.1, s32[2,4]{1,0:T(2,128)} %bitcast.2, f32[2,4]{1,0:T(2,128)} %bitcast.3, bf16[1,7168,512]{2,1,0:T(8,128)(2,1)} %wg_hbm.1, bf16[1,7168,512]{2,1,0:T(8,128)(2,1)} %wu_hbm.1, bf16[1,512,7168]{2,1,0:T(8,128)(2,1)} %wd_hbm.1), custom_call_target="tpu_custom_call" | custom-call | flops 1409286144 | bytes 22020096 | tf_op jit(solution)/shard_map/pallas_call | solution.py:245
  38.4 1.5 %copy.8 = bf16[4,7168]{1,0:T(4,128)(2,1)} copy(bf16[4,7168]{1,0:T(4,128)(2,1)} %shard_map.64) | data formatting | bytes 114688

commit v4 on v3

--- a/solution.py
+++ b/solution.py
@@ -43,7 +43,7 @@
     z, me = lax.axis_index("dp"), lax.axis_index("expert")
 
     zpeers = [modulo(z + i, groups) for i in range(1, groups)]
-    peers = [modulo(me + i, owners) for i in range(1, owners)]
+    peers = [modulo(me + i, owners) for i in (*range(2, owners - 1), 1, owners - 1)]
 
     def span_of(p, base=0):
         return pl.ds(pl.multiple_of(base + p * chunk, chunk), chunk)
@@ -57,6 +57,12 @@
 
     def arrive(ref, sem):
         pltpu.make_async_copy(ref, ref, sem).wait()
+
+    for at, (src, dst) in enumerate(((wg_hbm, wg), (wu_hbm, wu), (wd_hbm, wd))):
+        piece = dst.shape[0] // 4
+        for i in range(4):
+            span = pl.ds(i * piece, piece)
+            pltpu.make_async_copy(src.at[0, span, :], dst.at[span, :], wsem.at[at]).start()
 
     mine = tok[...].astype(F32)
     for p in range(parts):
@@ -82,12 +88,6 @@
         for to in zpeers:
             pltpu.make_async_remote_copy(
                 zbuf.at[p, z], zbuf.at[p, z], zs, zr.at[p], (to, me), device_id_type=MESH).start()
-    for at, (src, dst) in enumerate(((wg_hbm, wg), (wu_hbm, wu), (wd_hbm, wd))):
-        piece = dst.shape[0] // 4
-        for i in range(4):
-            span = pl.ds(i * piece, piece)
-            pltpu.make_async_copy(src.at[0, span, :], dst.at[span, :], wsem.at[at]).start()
-
     gate[...] = jnp.zeros_like(gate)
     up[...] = jnp.zeros_like(up)
 
@@ -120,28 +120,30 @@
     for u in range(halves):
         fits = (z_r == z_c) & (q_c == h_r * halves + u)
         sel_ref[u] = jnp.where(fits, chosen, 0.0).astype(BF16)
+
+    @pl.loop(0, parts)
+    def _(p):
+        arrive(zbuf.at[p, pl.ds(0, groups - 1)], zr.at[p])
+        tokens16 = zbuf[p].reshape(columns, small)
+        for u in range(halves):
+            picked = jnp.dot(sel_ref[u], tokens16, preferred_element_type=F32).astype(BF16)
+            outg[p, :, :, u * small : (u + 1) * small] = picked.reshape(
+                owners, tall, small)
+
+        for to in peers:
+            pltpu.make_async_remote_copy(
+                outg.at[p, to], arr.at[p, me], ps, pr.at[p],
+                (z, to), device_id_type=MESH).start()
+
+        arr[p, me] = outg[p, me]
+
+    for u in range(halves):
+        fits = (z_r == z_c) & (q_c == h_r * halves + u)
         back_weight = jnp.transpose(jnp.where(fits, weight, 0.0))
         high = back_weight.astype(BF16)
         low = (back_weight - high.astype(F32)).astype(BF16)
         comb_ref[u] = jnp.concatenate([high, low], axis=0)
 
-    @pl.loop(0, parts)
-    def _(p):
-        arrive(zbuf.at[p, pl.ds(0, groups - 1)], zr.at[p])
-        tokens16 = zbuf[p].reshape(columns, small)
-        for u in range(halves):
-            picked = jnp.dot(sel_ref[u], tokens16, preferred_element_type=F32).astype(BF16)
-            outg[:, :, pl.ds(pl.multiple_of(p * chunk + u * small, small), small)] = picked.reshape(
-                owners, tall, small)
-
-        span = span_of(p)
-        for to in peers:
-            pltpu.make_async_remote_copy(
-                outg.at[to, :, span], arr.at[me, :, span], ps, pr.at[p],
-                (z, to), device_id_type=MESH).start()
-
-        arr[me, :, span_of(p)] = outg[me, :, span_of(p)]
-
     some = min(owners, max(1, 128 // tall))
     blocks = owners // some
 
@@ -150,12 +152,12 @@
 
     @pl.loop(0, parts)
     def _(p):
-        arrive(arr.at[pl.ds(0, owners - 1), :, span_of(p)], pr.at[p])
+        arrive(arr.at[p, pl.ds(0, owners - 1)], pr.at[p])
 
         @pl.loop(0, blocks)
         def _(b):
             first = b * some
-            lhs = arr[pl.ds(first, some), :, span_of(p)].reshape(some * tall, chunk)
+            lhs = arr[p, pl.ds(first, some)].reshape(some * tall, chunk)
             at = pl.ds(pl.multiple_of(first * per, some * per), some * per)
             step = min(256, hidden)
             for mat, into in ((wg, gate), (wu, up)):
@@ -185,26 +187,25 @@
                     some, per, chunk)
                 for h in range(fold)
             ]
-            ret[pl.ds(first, some), :, span_of(p)] = jnp.concatenate(both, axis=1).astype(BF16)
-
-        span = span_of(p)
+            ret[p, pl.ds(first, some)] = jnp.concatenate(both, axis=1).astype(BF16)
+
         for to in peers:
             pltpu.make_async_remote_copy(
-                ret.at[to, :, span], back.at[me, :, span], rs, rr.at[p],
+                ret.at[p, to], back.at[p, me], rs, rr.at[p],
                 (z, to), device_id_type=MESH).start()
 
-        back[me, :, span_of(p)] = ret[me, :, span_of(p)]
+        back[p, me] = ret[p, me]
 
     arrive(mbuf.at[pl.ds(0, groups - 1)], ms)
     arrive(zbuf.at[:, pl.ds(0, groups - 1)], zs)
-    arrive(outg.at[pl.ds(0, owners - 1)], ps)
-
-    @pl.loop(0, parts)
-    def _(p):
-        arrive(back.at[pl.ds(0, owners - 1), :, span_of(p)], rr.at[p])
+    arrive(outg.at[:, pl.ds(0, owners - 1)], ps)
+
+    @pl.loop(0, parts)
+    def _(p):
+        arrive(back.at[p, pl.ds(0, owners - 1)], rr.at[p])
         mixed = jnp.zeros((columns, small), F32)
         for u in range(halves):
-            rhs = back[:, :, pl.ds(pl.multiple_of(p * chunk + u * small, small), small)]
+            rhs = back[p, :, :, u * small : (u + 1) * small]
             res = jnp.dot(comb_ref[u], rhs.reshape(total, small), preferred_element_type=F32)
             mixed = mixed + res[:columns] + res[columns:]
         acc[p] = mixed
@@ -216,7 +217,7 @@
 
         zin[p, z] = jnp.zeros((16, small), BF16)
 
-    arrive(ret.at[pl.ds(0, owners - 1)], rs)
+    arrive(ret.at[:, pl.ds(0, owners - 1)], rs)
     for p in range(parts):
         arrive(zin.at[p, pl.ds(0, groups - 1)], or_.at[p])
         own = acc[p, pl.ds(pl.multiple_of(z * 16, 16), 16), :]
@@ -254,8 +255,8 @@
         scratch_shapes=[
             vmem((width, hidden)), vmem((width, hidden)), vmem((hidden, width)),
             vmem((parts, groups, 16, small)), vmem((groups, 2 * rows * top, 128), F32),
-            vmem((owners, tall, wide)), vmem((owners, tall, wide)),
-            vmem((owners, tall, wide)), vmem((owners, tall, wide)),
+            vmem((parts, owners, tall, chunk)), vmem((parts, owners, tall, chunk)),
+            vmem((parts, owners, tall, chunk)), vmem((parts, owners, tall, chunk)),
             vmem((halves, total, columns)), vmem((halves, 2 * columns, total)),
             vmem((owners * per, hidden), F32), vmem((owners * per, hidden), F32),
             vmem((owners * per, hidden)), vmem((parts, columns, small), F32),

time: 40 us -> 40 us (level)
  no operation moved by 1% of the time
where the time goes in v4:
time: 40 us; the launch traced here: 39.8 us
  Pallas kernels  38.3 us (96%)
  local copies, waits for them, and re-layouts  1.46 us (4%)
    pallas_call x1, Pallas kernels, shards(): pl.pallas_call(functools.partial(kernel, sizes), out_shape=jax.ShapeDtype...  38.3 us
    unnamed x1, local copies, waits for them, and re-layouts  1.46 us

profile of v4, /device:TPU:0, one launch (start us, length us, event | category | flops | bytes accessed | tf_op | source)
XLA Modules:
  0.0 39.8 jit_solution(9612098024841355903)
XLA Ops:
  0.0 38.3 %shard_map.64 = bf16[4,7168]{1,0:T(4,128)(2,1)} custom-call(bf16[4,7168]{1,0:T(4,128)(2,1)} %tok.1, s32[2,4]{1,0:T(2,128)} %bitcast.2, f32[2,4]{1,0:T(2,128)} %bitcast.3, bf16[1,7168,512]{2,1,0:T(8,128)(2,1)} %wg_hbm.1, bf16[1,7168,512]{2,1,0:T(8,128)(2,1)} %wu_hbm.1, bf16[1,512,7168]{2,1,0:T(8,128)(2,1)} %wd_hbm.1), custom_call_target="tpu_custom_call" | custom-call | flops 1409286144 | bytes 22020096 | tf_op jit(solution)/shard_map/pallas_call | solution.py:246
  38.4 1.5 %copy.8 = bf16[4,7168]{1,0:T(4,128)(2,1)} copy(bf16[4,7168]{1,0:T(4,128)(2,1)} %shard_map.64) | data formatting | bytes 114688
